TPU v7x, 512 devices: a whole 4x4x16 slice. The times are simulated.
512 devices in a mesh: rows: 32 (over y, x, core), sub: 16 (over z).
Axes of the slice: x: 4, y: 4, z: 16, core: 2. Of those that a mesh axis runs over, the one named last changes fastest.
Arguments:
- knobs: float32 [48, 1048576], P(None, ('rows', 'sub')), may hold values from -6 to 6
- lengthscale: float32 [48], replicated, may hold values from 4 to 16
- earlier: float32 [256, 1048576], P(None, ('rows', 'sub')), may hold values from -0.06 to 0.06
- diagonal: float32 [1048576], P(('rows', 'sub')), may hold values from 1 to 2
- pivots: int32 [2, 128], replicated, may hold values from 0 to 1048575, as said below
Outputs:
- new_factor: float32 [256, 1048576], P(None, ('rows', 'sub'))
- residual_diag: float32 [1048576], P(('rows', 'sub'))
Inputs may be any that keep to these rules, and one draw needn't show every extreme that they name: All 256 ids are distinct row ids; the owners of the rows are chosen unevenly, some devices holding many pivots and most none.
All inputs are finite; a program needn't handle non-finite values.
Results may differ from a plain program's by a relative error of at most 0.0003.
Values sent between devices are 32-bit elements; how exact they have to be, the bound alone decides.
A program may use at most 64 MiB of HBM per device.

v0:
```python
import jax
import jax.numpy as jnp
from jax import lax
from jax.sharding import PartitionSpec as P


def kern(left, right_block, right_sq):
    cross_product = jnp.dot(
        left.T, right_block, precision=lax.Precision.HIGHEST, preferred_element_type=jnp.float32
    )
    lengthscale_square = jnp.sum(left * left, axis=0)
    return jnp.exp(-0.5 * (lengthscale_square[:, None] + right_sq[None, :] - 2.0 * cross_product))


def product(left, right_block):
    return jnp.dot(
        left.T, right_block, precision=lax.Precision.HIGHEST, preferred_element_type=jnp.float32
    )


def settle(piv, at_pivs):
    square = kern(piv, piv, jnp.sum(piv * piv, axis=0))
    for at_piv in at_pivs:
        square = square - product(at_piv, at_piv)
    square = square + 0.5 * jnp.eye(square.shape[0], dtype=jnp.float32)
    return jnp.linalg.cholesky(square)


def columns_of(lower, piv, at_pivs, targets, target_cols, target_sq):
    tile = kern(piv, targets, target_sq)
    for at_piv, cols in zip(at_pivs, target_cols):
        tile = tile - product(at_piv, cols)
    return lax.linalg.triangular_solve(lower, tile, left_side=True, lower=True)


def collect(tables):
    return lax.psum(tables, ("rows", "sub"))


def per_device(knobs, lengthscale, earlier, diagonal, pivots):
    count = knobs.shape[1]
    offset = (lax.axis_index("rows") * lax.axis_size("sub") + lax.axis_index("sub")) * count
    scaled = knobs / lengthscale[:, None]
    scaled_sq = jnp.sum(scaled * scaled, axis=0)

    def select(table, ids):
        local_ids = ids - offset
        owned = (local_ids >= 0) & (local_ids < count)
        taken = jnp.take(table, jnp.clip(local_ids, 0, count - 1), axis=1)
        return jnp.where(owned[None, :], taken, 0.0)

    piv_one, prev_one = collect((select(scaled, pivots[0]), select(earlier, pivots[0])))
    low_one = settle(piv_one, [prev_one])
    first = columns_of(low_one, piv_one, [prev_one], scaled, [earlier], scaled_sq)
    piv_two, prev_two, first_two = collect(
        (select(scaled, pivots[1]), select(earlier, pivots[1]), select(first, pivots[1]))
    )
    low_two = settle(piv_two, [prev_two, first_two])
    second = columns_of(
        low_two, piv_two, [prev_two, first_two], scaled, [earlier, first], scaled_sq
    )
    residual_diag = diagonal - jnp.sum(first * first, axis=0) - jnp.sum(second * second, axis=0)
    return (jnp.concatenate([first, second], axis=0), residual_diag)


def solution(mesh):
    in_specs = (P(None, ("rows", "sub")), P(), P(None, ("rows", "sub")), P(("rows", "sub")), P())
    out_specs = (P(None, ("rows", "sub")), P(("rows", "sub")))
    return jax.shard_map(
        per_device, mesh=mesh, in_specs=in_specs, out_specs=out_specs, check_vma=False
    )
```

profile of v0, /device:TPU:1, one launch (start us, length us, event | category | flops | bytes accessed | tf_op | source)
XLA Modules:
  0.0 984.2 jit_solution(18396560545731630008)
XLA Ops:
  7.2 0.8 and_bitcast_fusion
  8.0 0.8 compare_and_fusion
  8.8 2.0 copy.9
  10.8 0.8 gather_fusion.2
  12.4 1.3 copy.7
  13.7 1.6 multiply_reduce_fusion.2
  17.5 112.5 %all-reduce = (f32[48,128]{0,1:T(8,128)S(1)}, f32[48,128]{0,1:T(8,128)S(1)}) all-reduce(f32[48,128]{0,1:T(8,128)S(1)} %get-tuple-element.25, f32[48,128]{0,1:T(8,128)S(1)} %get-tuple-element.24), channel_id=1, replica_groups=mesh['rows'=32,'sub'=16] {'rows','sub'}, use_global_device_ids=true, to_apply=%region_0.2 | all-reduce | flops 12288 | bytes 98304 | tf_op jit(solution)/shard_map/psum | solution.py:37
  130.5 2.1 fusion.6
  132.6 2.2 fusion.3
  135.5 332.1 %all-reduce.5.cloned.1.call-done = f32[256,128]{0,1:T(8,128)} async-done(((f32[256,128]{0,1:T(8,128)}), f32[256,128]{0,1:T(8,128)}) %all-reduce.5.cloned.1.call-update) | async-done | bytes 131088 | tf_op jit(solution)/shard_map/psum | solution.py:37
  467.6 1.3 fusion.14
  469.0 11.7 %cholesky.44 = f32[128,128]{1,0:T(8,128)S(1)} custom-call(f32[128,128]{1,0:T(8,128)S(1)} %fusion.22), custom_call_target="Cholesky" | custom-call | tf_op jit(solution)/shard_map/jit(cholesky)/cholesky | solution.py:26
  482.0 9.8 custom-call.6
  491.9 2.5 convolution_subtract_fusion.1
  494.4 1.1 multiply_reduce_fusion.1
  495.5 1.3 copy.15
  496.8 1.9 gather_fusion
  499.7 444.9 %all-reduce.7.cloned.1.call-done = (f32[128,128]{1,0:T(8,128)}, f32[256,128]{0,1:T(8,128)}) async-done(((f32[128,128]{1,0:T(8,128)}, f32[256,128]{0,1:T(8,128)}), (f32[128,128]{1,0:T(8,128)}, f32[256,128]{0,1:T(8,128)})) %all-reduce.7.cloned.1.call-update) | async-done | bytes 196624 | tf_op jit(solution)/shard_map/psum | solution.py:37
  944.6 3.2 fusion.24
  948.5 11.7 %cholesky.55 = f32[128,128]{1,0:T(8,128)S(1)} custom-call(f32[128,128]{1,0:T(8,128)S(1)} %fusion.19), custom_call_target="Cholesky" | custom-call | tf_op jit(solution)/shard_map/jit(cholesky)/cholesky | solution.py:26
  961.5 9.8 custom-call.7
  971.4 2.8 fusion
  974.2 1.1 multiply_reduce_fusion
  975.3 1.5 pad_maximum_fusion
  (47 shorter events, 9.4 us)
Async XLA Ops:
  7.2 460.4 %all-reduce.5.cloned.1.call-start = ((), (), s32[]{:S(2)}) async-start(), calls=%async_computation | async-start | bytes 262144 | tf_op jit(solution)/shard_map/psum | solution.py:37
  8.8 3.6 copy-start.5
  8.8 3.6 copy-start.3
  10.8 3.0 copy-start.6
  12.3 932.3 %all-reduce.7.cloned.1.call-start = ((), (), s32[]{:S(2)}) async-start(), calls=%async_computation.1 | async-start | bytes 393216 | tf_op jit(solution)/shard_map/psum | solution.py:37
  132.6 359.2 %copy-start = (f32[256,2048]{1,0:T(8,128)S(1)}, f32[256,2048]{1,0:T(8,128)}, u32[]{:S(2)}) copy-start(f32[256,2048]{1,0:T(8,128)} %param.14) | copy-start | bytes 6291460
  944.6 3.2 copy-start.1
  944.6 3.5 copy-start.2
  975.3 1.5 copy-start.4
Sparse Core Ops, SparseCore 0:
  13.4 454.1 all-reduce.4
  499.6 444.9 all-reduce.6
where the time goes:
time: 985 us; the launch traced here: 984 us
  waiting for transfers between devices  777 us (79%)
  blocking collectives  112 us (11%)
  other arithmetic  53.4 us (5%)
  matrix products  17.4 us (2%)
  between operations  14.3 us (1%)
    psum x2, waiting for transfers between devices, collect(): return lax.psum(tables, ('rows', 'sub'))  777 us
    psum x1, blocking collectives, collect(): return lax.psum(tables, ('rows', 'sub'))  112 us
    another operation x6, other arithmetic, settle(): return jnp.linalg.cholesky(square)  24.8 us
    another operation x4, other arithmetic, columns_of(): return lax.linalg.triangular_solve(lower, tile, left_side=True, lower=True)  20.9 us
  transfers between devices with their start and end apart: 2, of which 2 were waited for; matrix products, arithmetic and copies ran while one was open for 1% of the time, Pallas kernels for 0%

commit v1 on v0

v1 whole, which is shorter than its diff:
```python
import jax
import jax.numpy as jnp
from jax import lax
from jax.experimental import pallas as pl
from jax.experimental.pallas import tpu as pltpu
from jax.sharding import PartitionSpec as P

MESH = pl.DeviceIdType.MESH
KNOBS, PREV, PIVOTS, LANES = 48, 256, 256, 128
TABLE = KNOBS + PREV
PIECES = 32
PIECE_ROWS = TABLE * (PIVOTS // LANES) // PIECES
CHUNK = 512
PANEL = 8
OUTER = 64
F32, BF16 = jnp.float32, jnp.bfloat16


def split_two(x):
    high = x.astype(BF16)
    return high, (x - high.astype(F32)).astype(BF16)


def split_three(x):
    high = x.astype(BF16)
    rest = x - high.astype(F32)
    mid = rest.astype(BF16)
    return high, mid, (rest - mid.astype(F32)).astype(BF16)


def dot(left, right, dims=((1,), (0,))):
    return lax.dot_general(left, right, (dims, ((), ())), preferred_element_type=F32)


def column_of(row):
    count = row.shape[1]
    square = jnp.broadcast_to(row, (count, count))
    same = lax.broadcasted_iota(jnp.int32, (count, count), 0) == lax.broadcasted_iota(
        jnp.int32, (count, count), 1
    )
    return jnp.sum(jnp.where(same, square, 0.0), axis=1, keepdims=True)


def select_kernel(ids_ref, ls_ref, knobs_ref, earlier_ref, out_ref, acc_ref):
    step = pl.program_id(0)
    width = knobs_ref.shape[1]
    count = width * pl.num_programs(0)
    device = lax.axis_index("rows") * lax.axis_size("sub") + lax.axis_index("sub")
    ids = jnp.concatenate([ids_ref[0:1, :], ids_ref[1:2, :]], axis=1) - (device * count + step * width)
    hot = jnp.where(lax.broadcasted_iota(jnp.int32, (width, PIVOTS), 0) == ids, 1.0, 0.0).astype(BF16)
    scaled = knobs_ref[...] / column_of(ls_ref[...])
    table = jnp.concatenate([scaled, earlier_ref[...]], axis=0)
    high, mid, low = split_three(table)
    found = dot(high, hot) + dot(mid, hot) + dot(low, hot)

    @pl.when(step == 0)
    def _():
        acc_ref[...] = found

    @pl.when(step > 0)
    def _():
        acc_ref[...] += found

    @pl.when(step == pl.num_programs(0) - 1)
    def _():
        for piece in range(PIECES):
            row, half = (piece // 2) * PIECE_ROWS, (piece % 2) * LANES
            out_ref[piece] = acc_ref[row : row + PIECE_ROWS, half : half + LANES]


def gather_kernel(part_ref, whole_ref, rows_in, near_in, far_in, near_out, far_out,
                  send_a, recv_a, send_b, recv_b, send_c, recv_c, send_d, recv_d):
    rows, sub = lax.axis_size("rows"), lax.axis_size("sub")
    row, z = lax.axis_index("rows"), lax.axis_index("sub")
    group = 4
    low, high = lax.rem(z, group), lax.div(z, group)

    def row_partner(k):
        return (lax.rem(row + k, rows), z)

    def near_partner(k):
        return (row, high * group + lax.rem(low + k, group))

    def far_partner(k):
        return (row, lax.rem(z + k * group, sub))

    barrier = pltpu.get_barrier_semaphore()

    def greet(k, _):
        pl.semaphore_signal(barrier, inc=1, device_id=row_partner(k), device_id_type=MESH)
        return _

    lax.fori_loop(1, rows, greet, 0)
    for k in range(1, group):
        pl.semaphore_signal(barrier, inc=1, device_id=near_partner(k), device_id_type=MESH)
        pl.semaphore_signal(barrier, inc=1, device_id=far_partner(k), device_id_type=MESH)
    pl.semaphore_wait(barrier, rows - 1 + 2 * (group - 1))

    def scatter(k):
        partner = row_partner(k)
        return pltpu.make_async_remote_copy(
            src_ref=part_ref.at[partner[0]], dst_ref=rows_in.at[k], send_sem=send_a.at[k],
            recv_sem=recv_a.at[k], device_id=partner, device_id_type=MESH)

    lax.fori_loop(1, rows, lambda k, c: (scatter(k).start(), c)[1], 0)
    lax.fori_loop(1, rows, lambda k, c: (scatter(k).wait_recv(), c)[1], 0)
    total = part_ref[row]
    for k in range(1, PIECES):
        total = total + rows_in[k]
    near_out[...] = total

    def near(k):
        return pltpu.make_async_remote_copy(
            src_ref=near_out, dst_ref=near_in.at[k], send_sem=send_b.at[k],
            recv_sem=recv_b.at[k], device_id=near_partner(k), device_id_type=MESH)

    for k in range(1, group):
        near(k).start()
    for k in range(1, group):
        near(k).wait_recv()
    total = near_out[...] + near_in[1] + near_in[2] + near_in[3]
    far_out[...] = total

    def far(k):
        return pltpu.make_async_remote_copy(
            src_ref=far_out, dst_ref=far_in.at[k], send_sem=send_c.at[k],
            recv_sem=recv_c.at[k], device_id=far_partner(k), device_id_type=MESH)

    for k in range(1, group):
        far(k).start()
    for k in range(1, group):
        far(k).wait_recv()
    whole_ref[row] = far_out[...] + far_in[1] + far_in[2] + far_in[3]

    def spread(k):
        return pltpu.make_async_remote_copy(
            src_ref=whole_ref.at[row], dst_ref=whole_ref.at[row], send_sem=send_d.at[k],
            recv_sem=recv_d.at[k], device_id=row_partner(k), device_id_type=MESH)

    def arrival(k):
        source = lax.rem(row + rows - k, rows)
        return pltpu.make_async_remote_copy(
            src_ref=whole_ref.at[source], dst_ref=whole_ref.at[source], send_sem=send_d.at[k],
            recv_sem=recv_d.at[k], device_id=row_partner(k), device_id_type=MESH)

    lax.fori_loop(1, rows, lambda k, c: (spread(k).start(), c)[1], 0)
    lax.fori_loop(1, rows, lambda k, c: (scatter(k).wait_send(), c)[1], 0)
    for k in range(1, group):
        near(k).wait_send()
        far(k).wait_send()
    lax.fori_loop(1, rows, lambda k, c: (arrival(k).wait_recv(), c)[1], 0)
    lax.fori_loop(1, rows, lambda k, c: (spread(k).wait_send(), c)[1], 0)


def extended(scaled, axis):
    square = -0.5 * jnp.sum(scaled * scaled, axis=axis, keepdims=True)
    pieces = [p.astype(F32) for p in split_three(square)]
    shape = tuple(16 if d == axis else s for d, s in enumerate(scaled.shape))
    place = lax.broadcasted_iota(jnp.int32, shape, axis)

    def rows(values):
        out = jnp.zeros(shape, F32)
        for i, value in enumerate(values):
            out = jnp.where(place == i, value, out)
        return out.astype(BF16)

    high, low = split_two(scaled)
    return high, low, rows, pieces


def left_form(scaled):
    high, low, rows, pieces = extended(scaled, 1)
    return jnp.concatenate([high, high, low, low, rows(pieces + [1.0, 1.0, 1.0])], axis=1)


def right_form(scaled):
    high, low, rows, pieces = extended(scaled, 0)
    return jnp.concatenate([high, low, high, low, rows([1.0, 1.0, 1.0] + pieces)], axis=0)


def tile_of(kern_left, prev_left, scaled, earlier):
    tile = jnp.exp(dot(kern_left[...], right_form(scaled)))
    high, low = split_two(earlier)
    prev_high = prev_left[0]
    return tile - (dot(prev_high, high) + (dot(prev_high, low) + dot(prev_left[1], high)))


def stacked(x, order):
    parts = split_three(x)
    return jnp.concatenate([parts[i] for i in order], axis=0)


LEFT_ORDER, RIGHT_ORDER = (0, 0, 1, 1, 0, 2), (0, 1, 0, 1, 2, 0)


def factor(aug):
    size = PIVOTS
    sub = lax.broadcasted_iota(jnp.int32, (PANEL, 1), 0)
    for start in range(0, size, OUTER):
        stop = start + OUTER
        for r in range(start, stop, PANEL):
            panel = aug[r : r + PANEL, :]
            for j in range(PANEL):
                pivot = panel[j : j + 1, r + j : r + j + 1]
                scale = lax.rsqrt(pivot)
                line = panel[j : j + 1, :] * scale
                below = jnp.where(sub > j, panel[:, r + j : r + j + 1] * scale, 0.0)
                panel = jnp.where(sub == j, line, panel - below * line)
            aug[r : r + PANEL, :] = panel
            if r + PANEL < stop:
                left = stacked(panel[:, : size], LEFT_ORDER)[:, r + PANEL : stop]
                aug[r + PANEL : stop, :] -= dot(left, stacked(panel, RIGHT_ORDER), ((0,), (0,)))
        if stop < size:
            block = aug[start:stop, :]
            high, low = split_two(block)
            left = jnp.concatenate([high, high, low, low], axis=0)[:, stop:size]
            right = jnp.concatenate([high, low, high, low], axis=0)
            aug[stop:size, :] -= dot(left, right, ((0,), (0,)))


def solve_kernel(whole_ref, ls_ref, knobs_ref, earlier_ref, diag_ref, out_ref, res_ref,
                 table, aug, kern_left, prev_left, inverse):
    step = pl.program_id(0)

    @pl.when(step == 0)
    def _():
        for piece in range(PIECES):
            row, half = (piece // 2) * PIECE_ROWS, (piece % 2) * LANES
            table[row : row + PIECE_ROWS, half : half + LANES] = whole_ref[piece]
        scaled = table[:KNOBS, :]
        earlier = table[KNOBS:, :]
        kern_left[...] = left_form(scaled.T)
        prev_left[0], prev_left[1] = split_two(earlier.T)
        eye = jnp.where(
            lax.broadcasted_iota(jnp.int32, (PIVOTS, PIVOTS), 0)
            == lax.broadcasted_iota(jnp.int32, (PIVOTS, PIVOTS), 1), 1.0, 0.0)
        aug[:, :PIVOTS] = tile_of(kern_left, prev_left, scaled, earlier) + 0.5 * eye
        aug[:, PIVOTS:] = eye
        factor(aug)
        inverse[0], inverse[1] = split_two(aug[:, PIVOTS:])

    scaled = knobs_ref[...] / column_of(ls_ref[...])
    tile = tile_of(kern_left, prev_left, scaled, earlier_ref[...])
    high, low = split_two(tile)
    inv_high = inverse[0]
    new = dot(inv_high, high) + (dot(inv_high, low) + dot(inverse[1], high))
    out_ref[...] = new
    res_ref[...] = diag_ref[...] - jnp.sum(new * new, axis=0, keepdims=True)


def gather(part):
    vmem = pl.BlockSpec(memory_space=pltpu.VMEM)
    slots = lambda n: pltpu.VMEM((n, PIECE_ROWS, LANES), F32)
    dma = pltpu.SemaphoreType.DMA
    return pl.pallas_call(
        gather_kernel,
        out_shape=jax.ShapeDtypeStruct(part.shape, F32),
        in_specs=[vmem],
        out_specs=vmem,
        scratch_shapes=[
            slots(PIECES), slots(4), slots(4),
            pltpu.VMEM((PIECE_ROWS, LANES), F32), pltpu.VMEM((PIECE_ROWS, LANES), F32),
            dma((PIECES,)), dma((PIECES,)), dma((4,)), dma((4,)),
            dma((4,)), dma((4,)), dma((PIECES,)), dma((PIECES,)),
        ],
        compiler_params=pltpu.CompilerParams(
            collective_id=0, has_side_effects=True, vmem_limit_bytes=8 << 20),
        name="gather_pivots",
    )(part)


def per_device(knobs, lengthscale, earlier, diagonal, pivots):
    count = knobs.shape[1]
    steps = count // CHUNK
    scale_row = lengthscale.reshape(1, KNOBS)
    piece_shape = (PIECES, PIECE_ROWS, LANES)
    fixed = lambda *shape: pl.BlockSpec(shape, lambda i: (0,) * len(shape))
    chunk = lambda rows: pl.BlockSpec((rows, CHUNK), lambda i: (0, i))
    part = pl.pallas_call(
        select_kernel,
        out_shape=jax.ShapeDtypeStruct(piece_shape, F32),
        grid=(steps,),
        in_specs=[fixed(2, LANES), fixed(1, KNOBS), chunk(KNOBS), chunk(PREV)],
        out_specs=fixed(*piece_shape),
        scratch_shapes=[pltpu.VMEM((TABLE, PIVOTS), F32)],
        compiler_params=pltpu.CompilerParams(vmem_limit_bytes=24 << 20),
        name="select_pivots",
    )(pivots, scale_row, knobs, earlier)
    whole = gather(part)
    new_factor, residual = pl.pallas_call(
        solve_kernel,
        out_shape=(
            jax.ShapeDtypeStruct((PIVOTS, count), F32),
            jax.ShapeDtypeStruct((1, count), F32),
        ),
        grid=(steps,),
        in_specs=[fixed(*piece_shape), fixed(1, KNOBS), chunk(KNOBS), chunk(PREV), chunk(1)],
        out_specs=(chunk(PIVOTS), chunk(1)),
        scratch_shapes=[
            pltpu.VMEM((TABLE, PIVOTS), F32),
            pltpu.VMEM((PIVOTS, 2 * PIVOTS), F32),
            pltpu.VMEM((PIVOTS, 4 * KNOBS + 16), BF16),
            pltpu.VMEM((2, PIVOTS, PREV), BF16),
            pltpu.VMEM((2, PIVOTS, PIVOTS), BF16),
        ],
        compiler_params=pltpu.CompilerParams(vmem_limit_bytes=24 << 20),
        name="solve_columns",
    )(whole, scale_row, knobs, earlier, diagonal.reshape(1, count))
    return new_factor, residual.reshape(count)


def solution(mesh):
    in_specs = (P(None, ("rows", "sub")), P(), P(None, ("rows", "sub")), P(("rows", "sub")), P())
    out_specs = (P(None, ("rows", "sub")), P(("rows", "sub")))
    return jax.shard_map(
        per_device, mesh=mesh, in_specs=in_specs, out_specs=out_specs, check_vma=False
    )
```

time: 985 us -> 80 us (0.08)
  waiting for transfers between devices: 777 us -> 0 us
  blocking collectives: 112 us -> 0 us
  Pallas kernels: 0 us -> 75.2 us
  other arithmetic: 53.4 us -> 0 us
  matrix products: 17.4 us -> 0 us
  between operations: 14.3 us -> 0.68 us
    psum x2 -> x0, waiting for transfers between devices: 777 us -> none  [collect(): return lax.psum(tables, ('rows', 'sub'))]
    psum x1 -> x0, blocking collectives: 112 us -> none  [collect(): return lax.psum(tables, ('rows', 'sub'))]
    pallas_call x0 -> x3, Pallas kernels: none -> 75.2 us  [the longest x1 40.4 us: gather(): pl.pallas_call(gather_kernel, out_shape=jax.ShapeDtypeStruct(part.shape,...]
    another operation x10 -> x0, other arithmetic: 45.7 us -> none  [the longest x6 24.8 us: settle(): return jnp.linalg.cholesky(square)]
    dot_general x10 -> x0, matrix products: 15.2 us -> none  [the longest x6 10.4 us: product(): jnp.dot(left.T, right_block, precision=lax.Precision.HIGHEST, preferred_e...]
  transfers between devices with their start and end apart: 2 -> 0, of which waited for: 2 -> 0; matrix products, arithmetic and copies ran while one was open for 1% -> 0% of each run, Pallas kernels for 0% -> 0%
where the time goes in v1:
time: 80 us; the launch traced here: 79.8 us
  Pallas kernels  75.2 us (94%)
  local copies, waits for them, and re-layouts  3.92 us (5%)
    pallas_call x1, Pallas kernels, gather(): pl.pallas_call(gather_kernel, out_shape=jax.ShapeDtypeStruct(part.shape,...  40.4 us
    pallas_call x1, Pallas kernels, per_device(): pl.pallas_call(solve_kernel, out_shape=(jax.ShapeDtypeStruct((PIVOTS, cou...  32.6 us
    unnamed x14, local copies, waits for them, and re-layouts  3.92 us
    pallas_call x1, Pallas kernels, per_device(): pl.pallas_call(select_kernel, out_shape=jax.ShapeDtypeStruct(piece_shape,...  2.28 us

profile of v1, /device:TPU:1, one launch (start us, length us, event | category | flops | bytes accessed | tf_op | source)
XLA Modules:
  0.0 79.8 jit_solution(4578086403079941003)
XLA Ops:
  0.6 0.0 copy-start
  0.6 1.6 %copy-done = f32[256,2048]{1,0:T(8,128)S(1)} copy-done((f32[256,2048]{1,0:T(8,128)S(1)}, f32[256,2048]{1,0:T(8,128)}, u32[]{:S(2)}) %copy-start) | copy-done | bytes 2097176
  2.2 0.0 copy-start.2
  2.2 1.0 %copy-done.2 = f32[48,2048]{1,0:T(8,128)S(1)} copy-done((f32[48,2048]{1,0:T(8,128)S(1)}, f32[48,2048]{1,0:T(8,128)}, u32[]{:S(2)}) %copy-start.2) | copy-done | bytes 393240
  3.2 0.0 copy-start.5
  3.2 0.7 copy-done.5
  3.9 0.0 copy-start.6
  3.9 0.7 copy-done.6
  4.6 0.0 copy-start.1
  4.6 0.0 copy-start.3
  4.6 0.0 copy-start.4
  4.6 2.3 %select_pivots.1.part_ref = f32[32,19,128]{2,1,0:T(8,128)S(1)} custom-call(s32[2,128]{1,0:T(2,128)S(1)} %copy-done.6, f32[1,48]{1,0:T(1,128)S(1)} %bitcast.4, f32[48,2048]{1,0:T(8,128)S(1)} %copy-done.2, f32[256,2048]{1,0:T(8,128)S(1)} %copy-done), custom_call_target="tpu_custom_call" | custom-call | tf_op jit(solution)/shard_map/select_pivots/pallas_call | solution.py:279
  6.9 40.4 %gather_pivots.1.whole_ref = f32[32,19,128]{2,1,0:T(8,128)S(1)} custom-call(f32[32,19,128]{2,1,0:T(8,128)S(1)} %select_pivots.1.part_ref), custom_call_target="tpu_custom_call" | custom-call | tf_op jit(solution)/shard_map/gather_pivots/pallas_call | solution.py:255
  47.2 0.0 copy-done.1
  47.2 0.0 copy-done.3
  47.3 0.0 copy-done.4
  47.3 32.6 %solve_columns.1 = (f32[256,2048]{1,0:T(8,128)}, f32[1,2048]{1,0:T(1,128)}) custom-call(f32[32,19,128]{2,1,0:T(8,128)S(1)} %gather_pivots.1.whole_ref, f32[1,48]{1,0:T(1,128)S(1)} %bitcast.5, f32[48,2048]{1,0:T(8,128)S(1)} %copy-done.3, f32[256,2048]{1,0:T(8,128)S(1)} %copy-done.1, f32[1,2048]{1,0:T(1,128)S(1)} %bitcast.3), custom_call_target="tpu_custom_call" | custom-call | tf_op jit(solution)/shard_map/solve_columns/pallas_call | solution.py:290
Async XLA Ops:
  0.6 1.6 %copy-start = (f32[256,2048]{1,0:T(8,128)S(1)}, f32[256,2048]{1,0:T(8,128)}, u32[]{:S(2)}) copy-start(f32[256,2048]{1,0:T(8,128)} %earlier_ref.3) | copy-start | bytes 6291460
  2.2 1.0 %copy-start.2 = (f32[48,2048]{1,0:T(8,128)S(1)}, f32[48,2048]{1,0:T(8,128)}, u32[]{:S(2)}) copy-start(f32[48,2048]{1,0:T(8,128)} %knobs_ref.3) | copy-start | bytes 1179652
  3.2 0.7 copy-start.5
  3.9 0.7 copy-start.6
  4.6 42.7 %copy-start.1 = (f32[256,2048]{1,0:T(8,128)S(1)}, f32[256,2048]{1,0:T(8,128)}, u32[]{:S(2)}) copy-start(f32[256,2048]{1,0:T(8,128)} %earlier_ref.3) | copy-start | bytes 6291460
  4.6 42.7 %copy-start.3 = (f32[48,2048]{1,0:T(8,128)S(1)}, f32[48,2048]{1,0:T(8,128)}, u32[]{:S(2)}) copy-start(f32[48,2048]{1,0:T(8,128)} %knobs_ref.3) | copy-start | bytes 1179652
  4.6 42.7 %copy-start.4 = (f32[2048]{0:T(1024)S(1)}, f32[2048]{0:T(1024)}, u32[]{:S(2)}) copy-start(f32[2048]{0:T(1024)} %param.8) | copy-start | bytes 24580

commit v2 on v1

v2 whole, which is shorter than its diff:
```python
import jax
import jax.numpy as jnp
from jax import lax
from jax.experimental import pallas as pl
from jax.experimental.pallas import tpu as pltpu
from jax.sharding import PartitionSpec as P

MESH = pl.DeviceIdType.MESH
KNOBS, PREV, PIVOTS, LANES = 48, 256, 256, 128
TABLE = KNOBS + PREV
PIECES = 32
PIECE_ROWS = TABLE * (PIVOTS // LANES) // PIECES
CHUNK = 512
GROUP, BLOCK = 8, 32
F32, BF16 = jnp.float32, jnp.bfloat16


def split_two(x):
    high = x.astype(BF16)
    return high, (x - high.astype(F32)).astype(BF16)


def split_three(x):
    high = x.astype(BF16)
    rest = x - high.astype(F32)
    mid = rest.astype(BF16)
    return high, mid, (rest - mid.astype(F32)).astype(BF16)


def dot(left, right, dims=((1,), (0,))):
    return lax.dot_general(left, right, (dims, ((), ())), preferred_element_type=F32)


def column_of(row):
    count = row.shape[1]
    square = jnp.broadcast_to(row, (count, count))
    same = lax.broadcasted_iota(jnp.int32, (count, count), 0) == lax.broadcasted_iota(
        jnp.int32, (count, count), 1
    )
    return jnp.sum(jnp.where(same, square, 0.0), axis=1, keepdims=True)


def ring(step, size):
    return min(step % size, -step % size)


AROUND = sorted(
    ((y, x, c) for y in range(4) for x in range(4) for c in range(2)),
    key=lambda t: -(4 * (ring(t[0], 4) + ring(t[1], 4)) + t[2]),
)[:-1]
NEAR, FAR, OPPOSITE = (-1, 1), (-3, 3, -6, 6), 8
ALONG = NEAR + (OPPOSITE,) + FAR
PARTS = 4


def collect_kernel(ids_hbm, ls_hbm, knobs_hbm, earlier_hbm, whole_ref, ids_ref, ls_ref, knobs, earlier, part, rows_in, z_in, z_out,
                   small_sem, load_sem, send_a, recv_a, send_z, recv_z, send_d, recv_d):
    row, z = lax.axis_index("rows"), lax.axis_index("sub")
    subs = lax.axis_size("sub")
    core, x0, y0 = lax.rem(row, 2), lax.rem(lax.div(row, 2), 4), lax.div(row, 8)
    count = knobs_hbm.shape[1]
    width = count // PARTS

    def load(i):
        columns = pl.ds(i * width, width)
        return [
            pltpu.make_async_copy(hbm.at[:, columns], vmem.at[:, columns], load_sem.at[j, i])
            for j, (hbm, vmem) in enumerate(((knobs_hbm, knobs), (earlier_hbm, earlier)))
        ]

    def around(t, sign=1):
        dy, dx, dc = t
        y, x = lax.rem(y0 + (dy * sign) % 4, 4), lax.rem(x0 + (dx * sign) % 4, 4)
        return (y * 4 + x) * 2 + (core + dc - 2 * core * dc)

    def along(d):
        return lax.rem(z + d % subs, subs)

    small = [
        pltpu.make_async_copy(hbm, vmem, small_sem.at[j])
        for j, (hbm, vmem) in enumerate(((ids_hbm, ids_ref), (ls_hbm, ls_ref)))
    ]
    for copy in small:
        copy.start()
    for i in range(PARTS):
        for copy in load(i):
            copy.start()
    barrier = pltpu.get_barrier_semaphore()
    for t in AROUND:
        pl.semaphore_signal(barrier, inc=1, device_id=(around(t), z), device_id_type=MESH)
    for d in ALONG:
        pl.semaphore_signal(barrier, inc=1, device_id=(row, along(d)), device_id_type=MESH)

    for copy in small:
        copy.wait()
    device = row * subs + z
    ids = jnp.concatenate([ids_ref[0:1, :], ids_ref[1:2, :]], axis=1) - device * count
    scale = column_of(ls_ref[...])
    table = None
    for i in range(PARTS):
        for copy in load(i):
            copy.wait()
        columns = pl.ds(i * width, width)
        hot = lax.broadcasted_iota(jnp.int32, (width, PIVOTS), 0) == ids - i * width
        hot = jnp.where(hot, 1.0, 0.0).astype(BF16)
        lines = jnp.concatenate([knobs[:, columns] / scale, earlier[:, columns]], axis=0)
        high, mid, low = split_three(lines)
        found = dot(high, hot) + dot(mid, hot) + dot(low, hot)
        table = found if table is None else table + found
    for piece in range(PIECES):
        top, half = (piece // 2) * PIECE_ROWS, (piece % 2) * LANES
        part[piece] = table[top : top + PIECE_ROWS, half : half + LANES]
    pl.semaphore_wait(barrier, len(AROUND) + len(ALONG))

    def scatter(i):
        target = around(AROUND[i])
        return pltpu.make_async_remote_copy(
            src_ref=part.at[target], dst_ref=rows_in.at[i], send_sem=send_a.at[i], recv_sem=recv_a.at[i],
            device_id=(target, z), device_id_type=MESH)

    def pass_on(i, source):
        return pltpu.make_async_remote_copy(
            src_ref=z_out.at[source], dst_ref=z_in.at[i], send_sem=send_z.at[i], recv_sem=recv_z.at[i],
            device_id=(row, along(ALONG[i])), device_id_type=MESH)

    def spread(i, source):
        return pltpu.make_async_remote_copy(
            src_ref=whole_ref.at[source], dst_ref=whole_ref.at[source], send_sem=send_d.at[i],
            recv_sem=recv_d.at[i], device_id=(around(AROUND[i]), z), device_id_type=MESH)

    others = range(len(AROUND))
    first, second = range(len(NEAR) + 1), range(len(NEAR) + 1, len(ALONG))
    for i in others:
        scatter(i).start()
    total = part[row]
    for i in reversed(others):
        scatter(i).wait_recv()
        total = total + rows_in[i]
    z_out[0] = total
    for i in first:
        pass_on(i, 0).start()
    for i in range(len(NEAR)):
        pass_on(i, 0).wait_recv()
        total = total + z_in[i]
    z_out[1] = total
    for i in second:
        pass_on(i, 1).start()
    for i in others:
        scatter(i).wait_send()
    for i in second:
        pass_on(i, 1).wait_recv()
        total = total + z_in[i]
    pass_on(len(NEAR), 0).wait_recv()
    whole_ref[row] = total + z_in[len(NEAR)]
    for i in others:
        spread(i, row).start()
    for i in first:
        pass_on(i, 0).wait_send()
    for i in second:
        pass_on(i, 1).wait_send()
    for i in reversed(others):
        spread(i, around(AROUND[i], -1)).wait_recv()
    for i in others:
        spread(i, row).wait_send()


def extended(scaled, axis):
    square = -0.5 * jnp.sum(scaled * scaled, axis=axis, keepdims=True)
    pieces = [p.astype(F32) for p in split_three(square)]
    shape = tuple(16 if d == axis else s for d, s in enumerate(scaled.shape))
    place = lax.broadcasted_iota(jnp.int32, shape, axis)

    def rows(values):
        out = jnp.zeros(shape, F32)
        for i, value in enumerate(values):
            out = jnp.where(place == i, value, out)
        return out.astype(BF16)

    high, low = split_two(scaled)
    return high, low, rows, pieces


def left_form(scaled):
    high, low, rows, pieces = extended(scaled, 1)
    return jnp.concatenate([high, high, low, low, rows(pieces + [1.0, 1.0, 1.0])], axis=1)


def right_form(scaled):
    high, low, rows, pieces = extended(scaled, 0)
    return jnp.concatenate([high, low, high, low, rows([1.0, 1.0, 1.0] + pieces)], axis=0)


def tile_of(kern_left, prev_left, scaled, earlier):
    tile = jnp.exp(dot(kern_left[...], right_form(scaled)))
    high, low = split_two(earlier)
    prev_high = prev_left[0]
    return tile - (dot(prev_high, high) + (dot(prev_high, low) + dot(prev_left[1], high)))


def factor(square):
    size = PIVOTS
    sub = lax.broadcasted_iota(jnp.int32, (GROUP, LANES), 0)
    sub_wide = lax.broadcasted_iota(jnp.int32, (GROUP, size), 0)
    lane_wide = lax.broadcasted_iota(jnp.int32, (GROUP, size), 1)
    full = lambda v: jnp.broadcast_to(v, (GROUP, LANES))
    wide = lambda v: jnp.concatenate([v] * (size // LANES), axis=1)
    groups = BLOCK // GROUP
    for start in range(0, size, BLOCK):
        stop = start + BLOCK
        lines = [square[start + GROUP * q : start + GROUP * q + GROUP, :] for q in range(groups)]
        for g in range(groups):
            first = start + GROUP * g
            below = range(g + 1, groups)
            cols = [
                {q: full(lines[q][:, first + k : first + k + 1]) for q in range(g, groups)} for k in range(GROUP)
            ]
            here = (lane_wide >= first) & (lane_wide < first + GROUP)
            for q in range(groups):
                fresh = jnp.where(lane_wide - first == sub_wide, 1.0, 0.0) if q == g else 0.0
                lines[q] = jnp.where(here, fresh, lines[q])
            for j in range(GROUP):
                scale = lax.rsqrt(full(cols[j][g][j : j + 1, :]))
                factors = {q: cols[j][q] * scale for q in below}
                factors[g] = jnp.where(sub > j, cols[j][g] * scale, 0.0)
                for k in range(j + 1, GROUP):
                    entry = full(cols[k][g][j : j + 1, :]) * scale
                    for q in range(g, groups):
                        cols[k][q] = cols[k][q] - factors[q] * entry
                line = jnp.broadcast_to(lines[g][j : j + 1, :], (GROUP, size)) * wide(scale)
                lines[g] = jnp.where(sub_wide == j, line, lines[g] - wide(factors[g]) * line)
                for q in below:
                    lines[q] = lines[q] - wide(factors[q]) * line
        block = jnp.concatenate(lines, axis=0)
        square[start:stop, :] = block
        if stop < size:
            high, low = split_two(block)
            left = jnp.concatenate([high, high, low, low], axis=0)[:, stop:]
            right = jnp.concatenate([high, low, high, low], axis=0)
            change = dot(left, right, ((0,), (0,)))
            lane = lax.broadcasted_iota(jnp.int32, (size - stop, size), 1)
            square[stop:, :] = jnp.where((lane >= start) & (lane < stop), 0.0, square[stop:, :]) - change


def solve_kernel(whole_ref, ls_ref, knobs_ref, earlier_ref, diag_ref, out_ref, res_ref,
                 table, square, kern_left, prev_left, inverse):
    step = pl.program_id(0)

    @pl.when(step == 0)
    def _():
        for piece in range(PIECES):
            row, half = (piece // 2) * PIECE_ROWS, (piece % 2) * LANES
            table[row : row + PIECE_ROWS, half : half + LANES] = whole_ref[piece]
        scaled = table[:KNOBS, :]
        earlier = table[KNOBS:, :]
        kern_left[...] = left_form(scaled.T)
        prev_left[0], prev_left[1] = split_two(earlier.T)
        eye = jnp.where(
            lax.broadcasted_iota(jnp.int32, (PIVOTS, PIVOTS), 0)
            == lax.broadcasted_iota(jnp.int32, (PIVOTS, PIVOTS), 1), 1.0, 0.0)
        square[...] = tile_of(kern_left, prev_left, scaled, earlier) + 0.5 * eye
        factor(square)
        lower = lax.broadcasted_iota(jnp.int32, (PIVOTS, PIVOTS), 0) >= lax.broadcasted_iota(
            jnp.int32, (PIVOTS, PIVOTS), 1)
        inverse[0], inverse[1] = split_two(jnp.where(lower, square[...], 0.0))

    scaled = knobs_ref[...] / column_of(ls_ref[...])
    tile = tile_of(kern_left, prev_left, scaled, earlier_ref[...])
    high, low = split_two(tile)
    inv_high = inverse[0]
    new = dot(inv_high, high) + (dot(inv_high, low) + dot(inverse[1], high))
    out_ref[...] = new
    res_ref[...] = diag_ref[...] - jnp.sum(new * new, axis=0, keepdims=True)


def collect(pivots, scale_row, knobs, earlier):
    vmem = pl.BlockSpec(memory_space=pltpu.VMEM)
    hbm = pl.BlockSpec(memory_space=pltpu.HBM)
    args = [pltpu.with_memory_space_constraint(a, pltpu.HBM) for a in (pivots, scale_row, knobs, earlier)]
    slots = lambda n: pltpu.VMEM((n, PIECE_ROWS, LANES), F32)
    dma = lambda *n: pltpu.SemaphoreType.DMA(n)
    others, chain = len(AROUND), len(ALONG)
    return pl.pallas_call(
        collect_kernel,
        out_shape=jax.ShapeDtypeStruct((PIECES, PIECE_ROWS, LANES), F32),
        in_specs=[hbm] * 4,
        out_specs=vmem,
        scratch_shapes=[
            pltpu.VMEM(pivots.shape, jnp.int32), pltpu.VMEM(scale_row.shape, F32),
            pltpu.VMEM(knobs.shape, F32), pltpu.VMEM(earlier.shape, F32),
            slots(PIECES), slots(others), slots(chain), slots(2), dma(2), dma(2, PARTS),
            dma(others), dma(others), dma(chain), dma(chain), dma(others), dma(others),
        ],
        compiler_params=pltpu.CompilerParams(
            collective_id=0, has_side_effects=True, vmem_limit_bytes=24 << 20),
        name="collect_pivots",
    )(*args)


def per_device(knobs, lengthscale, earlier, diagonal, pivots):
    count = knobs.shape[1]
    steps = count // CHUNK
    scale_row = lengthscale.reshape(1, KNOBS)
    piece_shape = (PIECES, PIECE_ROWS, LANES)
    fixed = lambda *shape: pl.BlockSpec(shape, lambda i: (0,) * len(shape))
    chunk = lambda rows: pl.BlockSpec((rows, CHUNK), lambda i: (0, i))
    whole = collect(pivots, scale_row, knobs, earlier)
    new_factor, residual = pl.pallas_call(
        solve_kernel,
        out_shape=(
            jax.ShapeDtypeStruct((PIVOTS, count), F32),
            jax.ShapeDtypeStruct((1, count), F32),
        ),
        grid=(steps,),
        in_specs=[fixed(*piece_shape), fixed(1, KNOBS), chunk(KNOBS), chunk(PREV), chunk(1)],
        out_specs=(chunk(PIVOTS), chunk(1)),
        scratch_shapes=[
            pltpu.VMEM((TABLE, PIVOTS), F32),
            pltpu.VMEM((PIVOTS, PIVOTS), F32),
            pltpu.VMEM((PIVOTS, 4 * KNOBS + 16), BF16),
            pltpu.VMEM((2, PIVOTS, PREV), BF16),
            pltpu.VMEM((2, PIVOTS, PIVOTS), BF16),
        ],
        compiler_params=pltpu.CompilerParams(vmem_limit_bytes=24 << 20),
        name="solve_columns",
    )(whole, scale_row, knobs, earlier, diagonal.reshape(1, count))
    return new_factor, residual.reshape(count)


def solution(mesh):
    in_specs = (P(None, ("rows", "sub")), P(), P(None, ("rows", "sub")), P(("rows", "sub")), P())
    out_specs = (P(None, ("rows", "sub")), P(("rows", "sub")))
    return jax.shard_map(
        per_device, mesh=mesh, in_specs=in_specs, out_specs=out_specs, check_vma=False
    )
```

time: 80 us -> 52.2 us (0.65)
  Pallas kernels: 75.2 us -> 51.4 us
  local copies, waits for them, and re-layouts: 3.92 us -> 0.02 us
    pallas_call x1, Pallas kernels: 32.6 us -> 13 us  [per_device(): pl.pallas_call(solve_kernel, out_shape=(jax.ShapeDtypeStruct((PIVOTS, cou...]
    pallas_call x2 -> x1, Pallas kernels: 42.7 us -> 38.4 us  [collect(): pl.pallas_call(collect_kernel, out_shape=jax.ShapeDtypeStruct((PIECES, PI...]
    unnamed x14 -> x8, local copies, waits for them, and re-layouts: 3.92 us -> 0.02 us
where the time goes in v2:
time: 52.2 us; the launch traced here: 52.1 us
  Pallas kernels  51.4 us (98%)
  between operations  0.7 us (1%)
    pallas_call x1, Pallas kernels, collect(): pl.pallas_call(collect_kernel, out_shape=jax.ShapeDtypeStruct((PIECES, PI...  38.4 us
    pallas_call x1, Pallas kernels, per_device(): pl.pallas_call(solve_kernel, out_shape=(jax.ShapeDtypeStruct((PIVOTS, cou...  13 us

profile of v2, /device:TPU:1, one launch (start us, length us, event | category | flops | bytes accessed | tf_op | source)
XLA Modules:
  0.0 52.1 jit_solution(14148113625652082289)
XLA Ops:
  0.6 0.0 copy-start
  0.6 0.0 copy-start.1
  0.7 0.0 copy-start.2
  0.7 0.0 copy-start.3
  0.7 38.4 %collect_pivots.1.whole_ref = f32[32,19,128]{2,1,0:T(8,128)S(1)} custom-call(s32[2,128]{1,0:T(2,128)} %ids_hbm.1, f32[1,48]{1,0:T(1,128)} %bitcast.4, f32[48,2048]{1,0:T(8,128)} %knobs_ref.1, f32[256,2048]{1,0:T(8,128)} %earlier_ref.1), custom_call_target="tpu_custom_call" | custom-call | tf_op jit(solution)/shard_map/collect_pivots/pallas_call | solution.py:282
  39.1 0.0 copy-done
  39.1 0.0 copy-done.1
  39.1 0.0 copy-done.2
  39.1 0.0 copy-done.3
  39.1 13.0 %solve_columns.1 = (f32[256,2048]{1,0:T(8,128)}, f32[1,2048]{1,0:T(1,128)}) custom-call(f32[32,19,128]{2,1,0:T(8,128)S(1)} %collect_pivots.1.whole_ref, f32[1,48]{1,0:T(1,128)S(1)} %bitcast.5, f32[48,2048]{1,0:T(8,128)S(1)} %copy-done.1, f32[256,2048]{1,0:T(8,128)S(1)} %copy-done, f32[1,2048]{1,0:T(1,128)S(1)} %bitcast.3), custom_call_target="tpu_custom_call" | custom-call | tf_op jit(solution)/shard_map/solve_columns/pallas_call | solution.py:307
Async XLA Ops:
  0.6 38.4 %copy-start = (f32[256,2048]{1,0:T(8,128)S(1)}, f32[256,2048]{1,0:T(8,128)}, u32[]{:S(2)}) copy-start(f32[256,2048]{1,0:T(8,128)} %earlier_ref.1) | copy-start | bytes 6291460
  0.6 38.4 %copy-start.1 = (f32[48,2048]{1,0:T(8,128)S(1)}, f32[48,2048]{1,0:T(8,128)}, u32[]{:S(2)}) copy-start(f32[48,2048]{1,0:T(8,128)} %knobs_ref.1) | copy-start | bytes 1179652
  0.7 38.4 %copy-start.2 = (f32[2048]{0:T(1024)S(1)}, f32[2048]{0:T(1024)}, u32[]{:S(2)}) copy-start(f32[2048]{0:T(1024)} %param.8) | copy-start | bytes 24580
  0.7 38.4 %copy-start.3 = (f32[48]{0:T(128)S(1)}, f32[48]{0:T(128)}, u32[]{:S(2)}) copy-start(f32[48]{0:T(128)} %param.6) | copy-start | bytes 580

commit v3 on v2

--- a/solution.py
+++ b/solution.py
@@ -8,10 +8,11 @@
 MESH = pl.DeviceIdType.MESH
 KNOBS, PREV, PIVOTS, LANES = 48, 256, 256, 128
 TABLE = KNOBS + PREV
+KERN_ROWS = 4 * KNOBS + 16
 PIECES = 32
 PIECE_ROWS = TABLE * (PIVOTS // LANES) // PIECES
 CHUNK = 512
-GROUP, BLOCK = 8, 32
+GROUP, WIDTH, BLOCK = 8, 16, 32
 F32, BF16 = jnp.float32, jnp.bfloat16
 
 
@@ -53,7 +54,8 @@
 PARTS = 4
 
 
-def collect_kernel(ids_hbm, ls_hbm, knobs_hbm, earlier_hbm, whole_ref, ids_ref, ls_ref, knobs, earlier, part, rows_in, z_in, z_out,
+def collect_kernel(ids_hbm, ls_hbm, knobs_hbm, earlier_hbm, whole_ref, kern_right, prev_right,
+                   ids_ref, ls_ref, knobs, earlier, part, rows_in, z_in, z_out,
                    small_sem, load_sem, send_a, recv_a, send_z, recv_z, send_d, recv_d):
     row, z = lax.axis_index("rows"), lax.axis_index("sub")
     subs = lax.axis_size("sub")
@@ -103,9 +105,13 @@
         columns = pl.ds(i * width, width)
         hot = lax.broadcasted_iota(jnp.int32, (width, PIVOTS), 0) == ids - i * width
         hot = jnp.where(hot, 1.0, 0.0).astype(BF16)
-        lines = jnp.concatenate([knobs[:, columns] / scale, earlier[:, columns]], axis=0)
-        high, mid, low = split_three(lines)
-        found = dot(high, hot) + dot(mid, hot) + dot(low, hot)
+        scaled = knobs[:, columns] / scale
+        knobs[:, columns] = scaled
+        high, low = split_two(scaled)
+        prev_high, prev_low = split_two(earlier[:, columns])
+        prev_right[0, :, columns], prev_right[1, :, columns] = prev_high, prev_low
+        high, low = jnp.concatenate([high, prev_high], axis=0), jnp.concatenate([low, prev_low], axis=0)
+        found = dot(high, hot) + dot(low, hot)
         table = found if table is None else table + found
     for piece in range(PIECES):
         top, half = (piece // 2) * PIECE_ROWS, (piece % 2) * LANES
@@ -132,6 +138,9 @@
     first, second = range(len(NEAR) + 1), range(len(NEAR) + 1, len(ALONG))
     for i in others:
         scatter(i).start()
+    for i in range(PARTS):
+        columns = pl.ds(i * width, width)
+        kern_right[:, columns] = right_form(knobs[:, columns])
     total = part[row]
     for i in reversed(others):
         scatter(i).wait_recv()
@@ -190,14 +199,13 @@
     return jnp.concatenate([high, low, high, low, rows([1.0, 1.0, 1.0] + pieces)], axis=0)
 
 
-def tile_of(kern_left, prev_left, scaled, earlier):
-    tile = jnp.exp(dot(kern_left[...], right_form(scaled)))
-    high, low = split_two(earlier)
-    prev_high = prev_left[0]
-    return tile - (dot(prev_high, high) + (dot(prev_high, low) + dot(prev_left[1], high)))
-
-
-def factor(square):
+def tile_of(kern_left, prev_left, kern_right, prev_high, prev_low):
+    tile = jnp.exp(dot(kern_left[...], kern_right))
+    left_high = prev_left[0]
+    return tile - (dot(left_high, prev_high) + (dot(left_high, prev_low) + dot(prev_left[1], prev_high)))
+
+
+def factor(square, between):
     size = PIVOTS
     sub = lax.broadcasted_iota(jnp.int32, (GROUP, LANES), 0)
     sub_wide = lax.broadcasted_iota(jnp.int32, (GROUP, size), 0)
@@ -208,27 +216,30 @@
     for start in range(0, size, BLOCK):
         stop = start + BLOCK
         lines = [square[start + GROUP * q : start + GROUP * q + GROUP, :] for q in range(groups)]
-        for g in range(groups):
-            first = start + GROUP * g
-            below = range(g + 1, groups)
+        for left in range(0, BLOCK, WIDTH):
+            first = start + left
             cols = [
-                {q: full(lines[q][:, first + k : first + k + 1]) for q in range(g, groups)} for k in range(GROUP)
+                {q: full(lines[q][:, first + k : first + k + 1]) for q in range((left + k) // GROUP, groups)}
+                for k in range(WIDTH)
             ]
-            here = (lane_wide >= first) & (lane_wide < first + GROUP)
+            here = (lane_wide >= first) & (lane_wide < first + WIDTH)
             for q in range(groups):
-                fresh = jnp.where(lane_wide - first == sub_wide, 1.0, 0.0) if q == g else 0.0
+                inside = left <= GROUP * q < left + WIDTH
+                fresh = jnp.where(lane_wide - start - GROUP * q == sub_wide, 1.0, 0.0) if inside else 0.0
                 lines[q] = jnp.where(here, fresh, lines[q])
-            for j in range(GROUP):
-                scale = lax.rsqrt(full(cols[j][g][j : j + 1, :]))
-                factors = {q: cols[j][q] * scale for q in below}
-                factors[g] = jnp.where(sub > j, cols[j][g] * scale, 0.0)
-                for k in range(j + 1, GROUP):
-                    entry = full(cols[k][g][j : j + 1, :]) * scale
-                    for q in range(g, groups):
+            for j in range(WIDTH):
+                g, at = (left + j) // GROUP, j % GROUP
+                scale = lax.rsqrt(full(cols[j][g][at : at + 1, :]))
+                factors = {q: cols[j][q] * scale for q in range(g, groups)}
+                factors[g] = jnp.where(sub > at, factors[g], 0.0)
+                for k in range(j + 1, WIDTH):
+                    own = (left + k) // GROUP
+                    entry = full(factors[own][k % GROUP : k % GROUP + 1, :])
+                    for q in range(own, groups):
                         cols[k][q] = cols[k][q] - factors[q] * entry
-                line = jnp.broadcast_to(lines[g][j : j + 1, :], (GROUP, size)) * wide(scale)
-                lines[g] = jnp.where(sub_wide == j, line, lines[g] - wide(factors[g]) * line)
-                for q in below:
+                line = jnp.broadcast_to(lines[g][at : at + 1, :], (GROUP, size)) * wide(scale)
+                lines[g] = jnp.where(sub_wide == at, line, lines[g] - wide(factors[g]) * line)
+                for q in range(g + 1, groups):
                     lines[q] = lines[q] - wide(factors[q]) * line
         block = jnp.concatenate(lines, axis=0)
         square[start:stop, :] = block
@@ -239,37 +250,43 @@
             change = dot(left, right, ((0,), (0,)))
             lane = lax.broadcasted_iota(jnp.int32, (size - stop, size), 1)
             square[stop:, :] = jnp.where((lane >= start) & (lane < stop), 0.0, square[stop:, :]) - change
-
-
-def solve_kernel(whole_ref, ls_ref, knobs_ref, earlier_ref, diag_ref, out_ref, res_ref,
-                 table, square, kern_left, prev_left, inverse):
-    step = pl.program_id(0)
-
-    @pl.when(step == 0)
-    def _():
-        for piece in range(PIECES):
-            row, half = (piece // 2) * PIECE_ROWS, (piece % 2) * LANES
-            table[row : row + PIECE_ROWS, half : half + LANES] = whole_ref[piece]
-        scaled = table[:KNOBS, :]
-        earlier = table[KNOBS:, :]
-        kern_left[...] = left_form(scaled.T)
-        prev_left[0], prev_left[1] = split_two(earlier.T)
-        eye = jnp.where(
-            lax.broadcasted_iota(jnp.int32, (PIVOTS, PIVOTS), 0)
-            == lax.broadcasted_iota(jnp.int32, (PIVOTS, PIVOTS), 1), 1.0, 0.0)
-        square[...] = tile_of(kern_left, prev_left, scaled, earlier) + 0.5 * eye
-        factor(square)
-        lower = lax.broadcasted_iota(jnp.int32, (PIVOTS, PIVOTS), 0) >= lax.broadcasted_iota(
-            jnp.int32, (PIVOTS, PIVOTS), 1)
-        inverse[0], inverse[1] = split_two(jnp.where(lower, square[...], 0.0))
-
-    scaled = knobs_ref[...] / column_of(ls_ref[...])
-    tile = tile_of(kern_left, prev_left, scaled, earlier_ref[...])
-    high, low = split_two(tile)
-    inv_high = inverse[0]
-    new = dot(inv_high, high) + (dot(inv_high, low) + dot(inverse[1], high))
-    out_ref[...] = new
-    res_ref[...] = diag_ref[...] - jnp.sum(new * new, axis=0, keepdims=True)
+        between(start // BLOCK)
+
+
+def solve_kernel(whole_ref, kern_right, prev_right, diag_ref, out_hbm, res_ref,
+                 table, square, kern_left, prev_left, tile, out_vmem, out_sem):
+    for piece in range(PIECES):
+        row, half = (piece // 2) * PIECE_ROWS, (piece % 2) * LANES
+        table[row : row + PIECE_ROWS, half : half + LANES] = whole_ref[piece]
+    scaled = table[:KNOBS, :]
+    high, low = split_two(table[KNOBS:, :])
+    kern_left[...] = left_form(scaled.T)
+    prev_left[0], prev_left[1] = split_two(table[KNOBS:, :].T)
+    rows = lax.broadcasted_iota(jnp.int32, (PIVOTS, PIVOTS), 0)
+    columns = lax.broadcasted_iota(jnp.int32, (PIVOTS, PIVOTS), 1)
+    at_pivots = tile_of(kern_left, prev_left, right_form(scaled), high, low)
+    square[...] = at_pivots + jnp.where(rows == columns, 0.5, 0.0)
+
+    count = out_hbm.shape[1]
+    width = count // (PIVOTS // BLOCK)
+
+    def between(b):
+        part = pl.ds(b * width, width)
+        tile[0, :, part], tile[1, :, part] = split_two(
+            tile_of(kern_left, prev_left, kern_right[:, part], prev_right[0, :, part], prev_right[1, :, part]))
+
+    factor(square, between)
+    inv_high, inv_low = split_two(jnp.where(rows >= columns, square[...], 0.0))
+    copies = []
+    for i in range(count // CHUNK):
+        part = pl.ds(i * CHUNK, CHUNK)
+        new = dot(inv_high, tile[0, :, part]) + (dot(inv_high, tile[1, :, part]) + dot(inv_low, tile[0, :, part]))
+        out_vmem[:, part] = new
+        copies.append(pltpu.make_async_copy(out_vmem.at[:, part], out_hbm.at[:, part], out_sem.at[i]))
+        copies[-1].start()
+        res_ref[:, part] = diag_ref[:, part] - jnp.sum(new * new, axis=0, keepdims=True)
+    for copy in copies:
+        copy.wait()
 
 
 def collect(pivots, scale_row, knobs, earlier):
@@ -281,9 +298,13 @@
     others, chain = len(AROUND), len(ALONG)
     return pl.pallas_call(
         collect_kernel,
-        out_shape=jax.ShapeDtypeStruct((PIECES, PIECE_ROWS, LANES), F32),
+        out_shape=(
+            jax.ShapeDtypeStruct((PIECES, PIECE_ROWS, LANES), F32),
+            jax.ShapeDtypeStruct((KERN_ROWS, knobs.shape[1]), BF16),
+            jax.ShapeDtypeStruct((2,) + earlier.shape, BF16),
+        ),
         in_specs=[hbm] * 4,
-        out_specs=vmem,
+        out_specs=(vmem,) * 3,
         scratch_shapes=[
             pltpu.VMEM(pivots.shape, jnp.int32), pltpu.VMEM(scale_row.shape, F32),
             pltpu.VMEM(knobs.shape, F32), pltpu.VMEM(earlier.shape, F32),
@@ -298,31 +319,28 @@
 
 def per_device(knobs, lengthscale, earlier, diagonal, pivots):
     count = knobs.shape[1]
-    steps = count // CHUNK
-    scale_row = lengthscale.reshape(1, KNOBS)
-    piece_shape = (PIECES, PIECE_ROWS, LANES)
-    fixed = lambda *shape: pl.BlockSpec(shape, lambda i: (0,) * len(shape))
-    chunk = lambda rows: pl.BlockSpec((rows, CHUNK), lambda i: (0, i))
-    whole = collect(pivots, scale_row, knobs, earlier)
+    whole, kern_right, prev_right = collect(pivots, lengthscale.reshape(1, KNOBS), knobs, earlier)
+    vmem = pl.BlockSpec(memory_space=pltpu.VMEM)
     new_factor, residual = pl.pallas_call(
         solve_kernel,
         out_shape=(
             jax.ShapeDtypeStruct((PIVOTS, count), F32),
             jax.ShapeDtypeStruct((1, count), F32),
         ),
-        grid=(steps,),
-        in_specs=[fixed(*piece_shape), fixed(1, KNOBS), chunk(KNOBS), chunk(PREV), chunk(1)],
-        out_specs=(chunk(PIVOTS), chunk(1)),
+        in_specs=[vmem] * 4,
+        out_specs=(pl.BlockSpec(memory_space=pltpu.HBM), vmem),
         scratch_shapes=[
             pltpu.VMEM((TABLE, PIVOTS), F32),
             pltpu.VMEM((PIVOTS, PIVOTS), F32),
-            pltpu.VMEM((PIVOTS, 4 * KNOBS + 16), BF16),
+            pltpu.VMEM((PIVOTS, KERN_ROWS), BF16),
             pltpu.VMEM((2, PIVOTS, PREV), BF16),
-            pltpu.VMEM((2, PIVOTS, PIVOTS), BF16),
+            pltpu.VMEM((2, PIVOTS, count), BF16),
+            pltpu.VMEM((PIVOTS, count), F32),
+            pltpu.SemaphoreType.DMA((count // CHUNK,)),
         ],
         compiler_params=pltpu.CompilerParams(vmem_limit_bytes=24 << 20),
         name="solve_columns",
-    )(whole, scale_row, knobs, earlier, diagonal.reshape(1, count))
+    )(whole, kern_right, prev_right, diagonal.reshape(1, count))
     return new_factor, residual.reshape(count)
 
 

time: 52.2 us -> 48.9 us (0.937)
  Pallas kernels: 51.4 us -> 48.1 us
    pallas_call x1, Pallas kernels: 13 us -> 9.81 us  [per_device(): pl.pallas_call(solve_kernel, out_shape=(jax.ShapeDtypeStruct((PIVOTS, cou...]
where the time goes in v3:
time: 48.9 us; the launch traced here: 48.8 us
  Pallas kernels  48.1 us (98%)
  between operations  0.65 us (1%)
    pallas_call x1, Pallas kernels, collect(): pl.pallas_call(collect_kernel, out_shape=(jax.ShapeDtypeStruct((PIECES, P...  38.3 us
    pallas_call x1, Pallas kernels, per_device(): pl.pallas_call(solve_kernel, out_shape=(jax.ShapeDtypeStruct((PIVOTS, cou...  9.81 us

profile of v3, /device:TPU:1, one launch (start us, length us, event | category | flops | bytes accessed | tf_op | source)
XLA Modules:
  0.0 48.8 jit_solution(127948077206551561)
XLA Ops:
  0.6 0.0 copy-start
  0.6 38.3 %collect_pivots.1 = (f32[32,19,128]{2,1,0:T(8,128)S(1)}, bf16[208,2048]{1,0:T(8,128)(2,1)S(1)}, bf16[2,256,2048]{2,1,0:T(8,128)(2,1)S(1)}) custom-call(s32[2,128]{1,0:T(2,128)} %ids_hbm.1, f32[1,48]{1,0:T(1,128)} %bitcast.4, f32[48,2048]{1,0:T(8,128)} %knobs_hbm.1, f32[256,2048]{1,0:T(8,128)} %earlier_hbm.1), custom_call_target="tpu_custom_call" | custom-call | tf_op jit(solution)/shard_map/collect_pivots/pallas_call | solution.py:299
  38.9 0.0 copy-done
  39.0 9.8 %solve_columns.1 = (f32[256,2048]{1,0:T(8,128)}, f32[1,2048]{1,0:T(1,128)}) custom-call(f32[32,19,128]{2,1,0:T(8,128)S(1)} %get-tuple-element.7.whole_ref, bf16[208,2048]{1,0:T(8,128)(2,1)S(1)} %get-tuple-element.8.kern_right, bf16[2,256,2048]{2,1,0:T(8,128)(2,1)S(1)} %get-tuple-element.9.prev_right, f32[1,2048]{1,0:T(1,128)S(1)} %bitcast.3), custom_call_target="tpu_custom_call" | custom-call | tf_op jit(solution)/shard_map/solve_columns/pallas_call | solution.py:324
Async XLA Ops:
  0.6 38.3 %copy-start = (f32[2048]{0:T(1024)S(1)}, f32[2048]{0:T(1024)}, u32[]{:S(2)}) copy-start(f32[2048]{0:T(1024)} %param.8) | copy-start | bytes 24580

commit v4 on v3

--- a/solution.py
+++ b/solution.py
@@ -51,7 +51,8 @@
 )[:-1]
 NEAR, FAR, OPPOSITE = (-1, 1), (-3, 3, -6, 6), 8
 ALONG = NEAR + (OPPOSITE,) + FAR
-PARTS = 4
+PARTS = 1
+EARLY_ROWS = ((0, 128, 4), (128, 192, 6))
 
 
 def collect_kernel(ids_hbm, ls_hbm, knobs_hbm, earlier_hbm, whole_ref, kern_right, prev_right,
@@ -138,8 +139,8 @@
     first, second = range(len(NEAR) + 1), range(len(NEAR) + 1, len(ALONG))
     for i in others:
         scatter(i).start()
-    for i in range(PARTS):
-        columns = pl.ds(i * width, width)
+    for i in range(count // CHUNK):
+        columns = pl.ds(i * CHUNK, CHUNK)
         kern_right[:, columns] = right_form(knobs[:, columns])
     total = part[row]
     for i in reversed(others):
@@ -212,6 +213,7 @@
     lane_wide = lax.broadcasted_iota(jnp.int32, (GROUP, size), 1)
     full = lambda v: jnp.broadcast_to(v, (GROUP, LANES))
     wide = lambda v: jnp.concatenate([v] * (size // LANES), axis=1)
+    entry = lambda column, row: full(column[row : row + 1, :])
     groups = BLOCK // GROUP
     for start in range(0, size, BLOCK):
         stop = start + BLOCK
@@ -227,20 +229,27 @@
                 inside = left <= GROUP * q < left + WIDTH
                 fresh = jnp.where(lane_wide - start - GROUP * q == sub_wide, 1.0, 0.0) if inside else 0.0
                 lines[q] = jnp.where(here, fresh, lines[q])
-            for j in range(WIDTH):
+            for j in range(0, WIDTH, 2):
                 g, at = (left + j) // GROUP, j % GROUP
-                scale = lax.rsqrt(full(cols[j][g][at : at + 1, :]))
-                factors = {q: cols[j][q] * scale for q in range(g, groups)}
-                factors[g] = jnp.where(sub > at, factors[g], 0.0)
-                for k in range(j + 1, WIDTH):
+                one, two = cols[j], cols[j + 1]
+                corner, side, last = entry(one[g], at), entry(one[g], at + 1), entry(two[g], at + 1)
+                scale_one = lax.rsqrt(corner)
+                both = scale_one * lax.rsqrt(corner * last - side * side)
+                scale_two = corner * both
+                one = {q: one[q] * scale_one for q in range(g, groups)}
+                two = {q: (two[q] * corner - cols[j][q] * side) * both for q in range(g, groups)}
+                one[g] = jnp.where(sub > at, one[g], 0.0)
+                two[g] = jnp.where(sub > at + 1, two[g], 0.0)
+                for k in range(j + 2, WIDTH):
                     own = (left + k) // GROUP
-                    entry = full(factors[own][k % GROUP : k % GROUP + 1, :])
+                    from_one, from_two = entry(one[own], k % GROUP), entry(two[own], k % GROUP)
                     for q in range(own, groups):
-                        cols[k][q] = cols[k][q] - factors[q] * entry
-                line = jnp.broadcast_to(lines[g][at : at + 1, :], (GROUP, size)) * wide(scale)
-                lines[g] = jnp.where(sub_wide == at, line, lines[g] - wide(factors[g]) * line)
-                for q in range(g + 1, groups):
-                    lines[q] = lines[q] - wide(factors[q]) * line
+                        cols[k][q] = cols[k][q] - (one[q] * from_one + two[q] * from_two)
+                for row, scale, factors in ((at, scale_one, one), (at + 1, scale_two, two)):
+                    line = jnp.broadcast_to(lines[g][row : row + 1, :], (GROUP, size)) * wide(scale)
+                    lines[g] = jnp.where(sub_wide == row, line, lines[g] - wide(factors[g]) * line)
+                    for q in range(g + 1, groups):
+                        lines[q] = lines[q] - wide(factors[q]) * line
         block = jnp.concatenate(lines, axis=0)
         square[start:stop, :] = block
         if stop < size:
@@ -268,23 +277,37 @@
     square[...] = at_pivots + jnp.where(rows == columns, 0.5, 0.0)
 
     count = out_hbm.shape[1]
-    width = count // (PIVOTS // BLOCK)
-
-    def between(b):
-        part = pl.ds(b * width, width)
+    copies = []
+
+    def tile_part(part):
         tile[0, :, part], tile[1, :, part] = split_two(
             tile_of(kern_left, prev_left, kern_right[:, part], prev_right[0, :, part], prev_right[1, :, part]))
 
+    def new_rows(top, stop, parts):
+        lower = rows[top:stop, :stop] >= columns[top:stop, :stop]
+        inv_high, inv_low = split_two(jnp.where(lower, square[top:stop, :stop], 0.0))
+        inv_both = jnp.concatenate([inv_high, inv_low], axis=0)
+        for part in parts:
+            both = dot(inv_both, tile[0, :stop, part])
+            new = both[: stop - top] + (dot(inv_high, tile[1, :stop, part]) + both[stop - top :])
+            out_vmem[top:stop, part] = new
+            copies.append(pltpu.make_async_copy(
+                out_vmem.at[top:stop, part], out_hbm.at[top:stop, part], out_sem.at[len(copies)]))
+            copies[-1].start()
+            rest = diag_ref[:, part] if top == 0 else res_ref[:, part]
+            res_ref[:, part] = rest - jnp.sum(new * new, axis=0, keepdims=True)
+
+    parts = [pl.ds(i * CHUNK, CHUNK) for i in range(count // CHUNK)]
+
+    def between(b):
+        if b < len(parts):
+            tile_part(parts[b])
+        for top, stop, after in EARLY_ROWS:
+            if b == after:
+                new_rows(top, stop, parts)
+
     factor(square, between)
-    inv_high, inv_low = split_two(jnp.where(rows >= columns, square[...], 0.0))
-    copies = []
-    for i in range(count // CHUNK):
-        part = pl.ds(i * CHUNK, CHUNK)
-        new = dot(inv_high, tile[0, :, part]) + (dot(inv_high, tile[1, :, part]) + dot(inv_low, tile[0, :, part]))
-        out_vmem[:, part] = new
-        copies.append(pltpu.make_async_copy(out_vmem.at[:, part], out_hbm.at[:, part], out_sem.at[i]))
-        copies[-1].start()
-        res_ref[:, part] = diag_ref[:, part] - jnp.sum(new * new, axis=0, keepdims=True)
+    new_rows(EARLY_ROWS[-1][1], PIVOTS, parts)
     for copy in copies:
         copy.wait()
 
@@ -336,7 +359,7 @@
             pltpu.VMEM((2, PIVOTS, PREV), BF16),
             pltpu.VMEM((2, PIVOTS, count), BF16),
             pltpu.VMEM((PIVOTS, count), F32),
-            pltpu.SemaphoreType.DMA((count // CHUNK,)),
+            pltpu.SemaphoreType.DMA(((len(EARLY_ROWS) + 1) * (count // CHUNK),)),
         ],
         compiler_params=pltpu.CompilerParams(vmem_limit_bytes=24 << 20),
         name="solve_columns",

time: 48.9 us -> 47.5 us (0.971)
  Pallas kernels: 48.1 us -> 46.7 us
    pallas_call x1, Pallas kernels: 9.81 us -> 8.46 us  [per_device(): pl.pallas_call(solve_kernel, out_shape=(jax.ShapeDtypeStruct((PIVOTS, cou...]
where the time goes in v4:
time: 47.5 us; the launch traced here: 47.3 us
  Pallas kernels  46.7 us (98%)
  between operations  0.65 us (1%)
    pallas_call x1, Pallas kernels, collect(): pl.pallas_call(collect_kernel, out_shape=(jax.ShapeDtypeStruct((PIECES, P...  38.2 us
    pallas_call x1, Pallas kernels, per_device(): pl.pallas_call(solve_kernel, out_shape=(jax.ShapeDtypeStruct((PIVOTS, cou...  8.46 us

profile of v4, /device:TPU:1, one launch (start us, length us, event | category | flops | bytes accessed | tf_op | source)
XLA Modules:
  0.0 47.3 jit_solution(1731730676907079547)
XLA Ops:
  0.6 0.0 copy-start
  0.6 38.2 %collect_pivots.1 = (f32[32,19,128]{2,1,0:T(8,128)S(1)}, bf16[208,2048]{1,0:T(8,128)(2,1)S(1)}, bf16[2,256,2048]{2,1,0:T(8,128)(2,1)S(1)}) custom-call(s32[2,128]{1,0:T(2,128)} %ids_hbm.1, f32[1,48]{1,0:T(1,128)} %bitcast.4, f32[48,2048]{1,0:T(8,128)} %knobs_hbm.1, f32[256,2048]{1,0:T(8,128)} %earlier_hbm.1), custom_call_target="tpu_custom_call" | custom-call | tf_op jit(solution)/shard_map/collect_pivots/pallas_call | solution.py:322
  38.9 0.0 copy-done
  38.9 8.5 %solve_columns.1 = (f32[256,2048]{1,0:T(8,128)}, f32[1,2048]{1,0:T(1,128)}) custom-call(f32[32,19,128]{2,1,0:T(8,128)S(1)} %get-tuple-element.7.whole_ref, bf16[208,2048]{1,0:T(8,128)(2,1)S(1)} %get-tuple-element.8.kern_right, bf16[2,256,2048]{2,1,0:T(8,128)(2,1)S(1)} %get-tuple-element.9.prev_right, f32[1,2048]{1,0:T(1,128)S(1)} %bitcast.3), custom_call_target="tpu_custom_call" | custom-call | tf_op jit(solution)/shard_map/solve_columns/pallas_call | solution.py:347
Async XLA Ops:
  0.6 38.2 %copy-start = (f32[2048]{0:T(1024)S(1)}, f32[2048]{0:T(1024)}, u32[]{:S(2)}) copy-start(f32[2048]{0:T(1024)} %param.8) | copy-start | bytes 24580

commit v5 on v4

--- a/solution.py
+++ b/solution.py
@@ -175,7 +175,9 @@
 
 
 def extended(scaled, axis):
-    square = -0.5 * jnp.sum(scaled * scaled, axis=axis, keepdims=True)
+    high, low = split_two(scaled)
+    held = high.astype(F32) + low.astype(F32)
+    square = -0.5 * jnp.sum(held * held, axis=axis, keepdims=True)
     pieces = [p.astype(F32) for p in split_three(square)]
     shape = tuple(16 if d == axis else s for d, s in enumerate(scaled.shape))
     place = lax.broadcasted_iota(jnp.int32, shape, axis)
@@ -186,7 +188,6 @@
             out = jnp.where(place == i, value, out)
         return out.astype(BF16)
 
-    high, low = split_two(scaled)
     return high, low, rows, pieces
 
 
@@ -280,16 +281,17 @@
     copies = []
 
     def tile_part(part):
-        tile[0, :, part], tile[1, :, part] = split_two(
+        tile[0, :, part], tile[1, :, part], tile[2, :, part] = split_three(
             tile_of(kern_left, prev_left, kern_right[:, part], prev_right[0, :, part], prev_right[1, :, part]))
 
     def new_rows(top, stop, parts):
         lower = rows[top:stop, :stop] >= columns[top:stop, :stop]
-        inv_high, inv_low = split_two(jnp.where(lower, square[top:stop, :stop], 0.0))
-        inv_both = jnp.concatenate([inv_high, inv_low], axis=0)
+        inverse = split_three(jnp.where(lower, square[top:stop, :stop], 0.0))
+        inv_high, inv_both = inverse[0], jnp.concatenate(inverse, axis=0)
         for part in parts:
-            both = dot(inv_both, tile[0, :stop, part])
-            new = both[: stop - top] + (dot(inv_high, tile[1, :stop, part]) + both[stop - top :])
+            both, rest = dot(inv_both, tile[0, :stop, part]), dot(inv_both[: 2 * (stop - top)], tile[1, :stop, part])
+            n = stop - top
+            new = both[:n] + ((both[n : 2 * n] + rest[:n]) + (both[2 * n :] + rest[n:] + dot(inv_high, tile[2, :stop, part])))
             out_vmem[top:stop, part] = new
             copies.append(pltpu.make_async_copy(
                 out_vmem.at[top:stop, part], out_hbm.at[top:stop, part], out_sem.at[len(copies)]))
@@ -357,7 +359,7 @@
             pltpu.VMEM((PIVOTS, PIVOTS), F32),
             pltpu.VMEM((PIVOTS, KERN_ROWS), BF16),
             pltpu.VMEM((2, PIVOTS, PREV), BF16),
-            pltpu.VMEM((2, PIVOTS, count), BF16),
+            pltpu.VMEM((3, PIVOTS, count), BF16),
             pltpu.VMEM((PIVOTS, count), F32),
             pltpu.SemaphoreType.DMA(((len(EARLY_ROWS) + 1) * (count // CHUNK),)),
         ],

time: 47.5 us -> 47.7 us (level)
  no operation moved by 1% of the time
where the time goes in v5:
time: 47.7 us; the launch traced here: 47.5 us
  Pallas kernels  46.9 us (98%)
  between operations  0.65 us (1%)
    pallas_call x1, Pallas kernels, collect(): pl.pallas_call(collect_kernel, out_shape=(jax.ShapeDtypeStruct((PIECES, P...  38.2 us
    pallas_call x1, Pallas kernels, per_device(): pl.pallas_call(solve_kernel, out_shape=(jax.ShapeDtypeStruct((PIVOTS, cou...  8.65 us

profile of v5, /device:TPU:1, one launch (start us, length us, event | category | flops | bytes accessed | tf_op | source)
XLA Modules:
  0.0 47.5 jit_solution(13644897047203371853)
XLA Ops:
  0.6 0.0 copy-start
  0.6 38.2 %collect_pivots.1 = (f32[32,19,128]{2,1,0:T(8,128)S(1)}, bf16[208,2048]{1,0:T(8,128)(2,1)S(1)}, bf16[2,256,2048]{2,1,0:T(8,128)(2,1)S(1)}) custom-call(s32[2,128]{1,0:T(2,128)} %ids_hbm.1, f32[1,48]{1,0:T(1,128)} %bitcast.4, f32[48,2048]{1,0:T(8,128)} %knobs_hbm.1, f32[256,2048]{1,0:T(8,128)} %earlier_hbm.1), custom_call_target="tpu_custom_call" | custom-call | tf_op jit(solution)/shard_map/collect_pivots/pallas_call | solution.py:324
  38.9 0.0 copy-done
  38.9 8.6 %solve_columns.1 = (f32[256,2048]{1,0:T(8,128)}, f32[1,2048]{1,0:T(1,128)}) custom-call(f32[32,19,128]{2,1,0:T(8,128)S(1)} %get-tuple-element.7.whole_ref, bf16[208,2048]{1,0:T(8,128)(2,1)S(1)} %get-tuple-element.8.kern_right, bf16[2,256,2048]{2,1,0:T(8,128)(2,1)S(1)} %get-tuple-element.9.prev_right, f32[1,2048]{1,0:T(1,128)S(1)} %bitcast.3), custom_call_target="tpu_custom_call" | custom-call | tf_op jit(solution)/shard_map/solve_columns/pallas_call | solution.py:349
Async XLA Ops:
  0.6 38.2 %copy-start = (f32[2048]{0:T(1024)S(1)}, f32[2048]{0:T(1024)}, u32[]{:S(2)}) copy-start(f32[2048]{0:T(1024)} %param.8) | copy-start | bytes 24580

commit v6 on v5

--- a/solution.py
+++ b/solution.py
@@ -49,10 +49,11 @@
     ((y, x, c) for y in range(4) for x in range(4) for c in range(2)),
     key=lambda t: -(4 * (ring(t[0], 4) + ring(t[1], 4)) + t[2]),
 )[:-1]
-NEAR, FAR, OPPOSITE = (-1, 1), (-3, 3, -6, 6), 8
-ALONG = NEAR + (OPPOSITE,) + FAR
+NEAR, FAR = (1, -1, -2), (6, 3, -3, -6)
+ALONG = NEAR + FAR
+GREET = (1, -1, 2, -2, 3, -3, 6, -6)
 PARTS = 1
-EARLY_ROWS = ((0, 128, 4), (128, 192, 6))
+EARLY_ROWS = ((0, 128, 4), (128, 224, 6))
 
 
 def collect_kernel(ids_hbm, ls_hbm, knobs_hbm, earlier_hbm, whole_ref, kern_right, prev_right,
@@ -91,7 +92,7 @@
     barrier = pltpu.get_barrier_semaphore()
     for t in AROUND:
         pl.semaphore_signal(barrier, inc=1, device_id=(around(t), z), device_id_type=MESH)
-    for d in ALONG:
+    for d in GREET:
         pl.semaphore_signal(barrier, inc=1, device_id=(row, along(d)), device_id_type=MESH)
 
     for copy in small:
@@ -117,7 +118,7 @@
     for piece in range(PIECES):
         top, half = (piece // 2) * PIECE_ROWS, (piece % 2) * LANES
         part[piece] = table[top : top + PIECE_ROWS, half : half + LANES]
-    pl.semaphore_wait(barrier, len(AROUND) + len(ALONG))
+    pl.semaphore_wait(barrier, len(AROUND) + len(GREET))
 
     def scatter(i):
         target = around(AROUND[i])
@@ -136,7 +137,7 @@
             recv_sem=recv_d.at[i], device_id=(around(AROUND[i]), z), device_id_type=MESH)
 
     others = range(len(AROUND))
-    first, second = range(len(NEAR) + 1), range(len(NEAR) + 1, len(ALONG))
+    first, second = range(len(NEAR)), range(len(NEAR), len(ALONG))
     for i in others:
         scatter(i).start()
     for i in range(count // CHUNK):
@@ -149,25 +150,27 @@
     z_out[0] = total
     for i in first:
         pass_on(i, 0).start()
-    for i in range(len(NEAR)):
+    for i in first[:-1]:
         pass_on(i, 0).wait_recv()
         total = total + z_in[i]
     z_out[1] = total
-    for i in second:
+    for i in second[:-1]:
         pass_on(i, 1).start()
+    pass_on(first[-1], 0).wait_recv()
+    z_out[2] = total + z_in[first[-1]]
+    pass_on(second[-1], 2).start()
     for i in others:
         scatter(i).wait_send()
     for i in second:
         pass_on(i, 1).wait_recv()
         total = total + z_in[i]
-    pass_on(len(NEAR), 0).wait_recv()
-    whole_ref[row] = total + z_in[len(NEAR)]
+    whole_ref[row] = total
     for i in others:
         spread(i, row).start()
     for i in first:
         pass_on(i, 0).wait_send()
     for i in second:
-        pass_on(i, 1).wait_send()
+        pass_on(i, 2 if i == second[-1] else 1).wait_send()
     for i in reversed(others):
         spread(i, around(AROUND[i], -1)).wait_recv()
     for i in others:
@@ -333,7 +336,7 @@
         scratch_shapes=[
             pltpu.VMEM(pivots.shape, jnp.int32), pltpu.VMEM(scale_row.shape, F32),
             pltpu.VMEM(knobs.shape, F32), pltpu.VMEM(earlier.shape, F32),
-            slots(PIECES), slots(others), slots(chain), slots(2), dma(2), dma(2, PARTS),
+            slots(PIECES), slots(others), slots(chain), slots(3), dma(2), dma(2, PARTS),
             dma(others), dma(others), dma(chain), dma(chain), dma(others), dma(others),
         ],
         compiler_params=pltpu.CompilerParams(

time: 47.7 us -> 47.5 us (level)
  no operation moved by 1% of the time
where the time goes in v6:
time: 47.5 us; the launch traced here: 47.4 us
  Pallas kernels  46.7 us (98%)
  between operations  0.65 us (1%)
    pallas_call x1, Pallas kernels, collect(): pl.pallas_call(collect_kernel, out_shape=(jax.ShapeDtypeStruct((PIECES, P...  38.1 us
    pallas_call x1, Pallas kernels, per_device(): pl.pallas_call(solve_kernel, out_shape=(jax.ShapeDtypeStruct((PIVOTS, cou...  8.58 us

profile of v6, /device:TPU:1, one launch (start us, length us, event | category | flops | bytes accessed | tf_op | source)
XLA Modules:
  0.0 47.4 jit_solution(16770975529606427435)
XLA Ops:
  0.6 0.0 copy-start
  0.6 38.1 %collect_pivots.1 = (f32[32,19,128]{2,1,0:T(8,128)S(1)}, bf16[208,2048]{1,0:T(8,128)(2,1)S(1)}, bf16[2,256,2048]{2,1,0:T(8,128)(2,1)S(1)}) custom-call(s32[2,128]{1,0:T(2,128)} %ids_hbm.1, f32[1,48]{1,0:T(1,128)} %bitcast.4, f32[48,2048]{1,0:T(8,128)} %knobs_hbm.1, f32[256,2048]{1,0:T(8,128)} %earlier_hbm.1), custom_call_target="tpu_custom_call" | custom-call | tf_op jit(solution)/shard_map/collect_pivots/pallas_call | solution.py:327
  38.8 0.0 copy-done
  38.8 8.6 %solve_columns.1 = (f32[256,2048]{1,0:T(8,128)}, f32[1,2048]{1,0:T(1,128)}) custom-call(f32[32,19,128]{2,1,0:T(8,128)S(1)} %get-tuple-element.7.whole_ref, bf16[208,2048]{1,0:T(8,128)(2,1)S(1)} %get-tuple-element.8.kern_right, bf16[2,256,2048]{2,1,0:T(8,128)(2,1)S(1)} %get-tuple-element.9.prev_right, f32[1,2048]{1,0:T(1,128)S(1)} %bitcast.3), custom_call_target="tpu_custom_call" | custom-call | tf_op jit(solution)/shard_map/solve_columns/pallas_call | solution.py:352
Async XLA Ops:
  0.6 38.2 %copy-start = (f32[2048]{0:T(1024)S(1)}, f32[2048]{0:T(1024)}, u32[]{:S(2)}) copy-start(f32[2048]{0:T(1024)} %param.8) | copy-start | bytes 24580
